TPU v7x, 32 devices: a whole 2x2x4 slice. The times are simulated.
32 devices in a mesh: dp: 8 (over z, x), mp: 4 (over y, core).
Axes of the slice: x: 2, y: 2, z: 4, core: 2. Of those that a mesh axis runs over, the one named last changes fastest.
Arguments:
- byte_ids: int32 [32, 2048], P('dp'), may hold values from 0 to 261
- lengths: int32 [32], P('dp'), may hold values from 512 to 2048, as said below
- latents: bfloat16 [32, 256, 1280], P('dp'), may hold values from -6 to 6
- byte_table: bfloat16 [262, 768], replicated, may hold values from -6 to 6
- pos_table: bfloat16 [2048, 768], replicated, may hold values from -3 to 3
- gain_in: float32 [768], replicated, may hold values from 0.25 to 1.75
- gain_lat: float32 [1280], replicated, may hold values from 0.25 to 1.75
- gain_mlp: float32 [1280], replicated, may hold values from 0.25 to 1.75
- w_query: bfloat16 [1280, 256], P(None, 'mp'), may hold values from -0.15625 to 0.15625
- w_key: bfloat16 [768, 256], P(None, 'mp'), may hold values from -0.21875 to 0.21875
- w_value: bfloat16 [768, 1280], P(None, 'mp'), may hold values from -0.21875 to 0.21875
- w_out: bfloat16 [1280, 1280], P('mp'), may hold values from -4 to 4
- w_one: bfloat16 [1280, 1280], P(None, 'mp'), may hold values from -0.15625 to 0.15625
- w_two: bfloat16 [1280, 1280], P('mp'), may hold values from -0.15625 to 0.15625
- out_grad: bfloat16 [32, 256, 1280], P('dp'), may hold values from -6 to 6
Outputs:
- latents_out: bfloat16 [32, 256, 1280], P('dp')
- latent_grad: float32 [32, 256, 1280], P('dp')
- byte_grad: float32 [262, 768], P(None, 'mp')
- pos_grad: float32 [2048, 768], P('dp', 'mp')
- gain_in_grad: float32 [768], P('mp')
- gain_lat_grad: float32 [1280], P('mp')
- gain_mlp_grad: float32 [1280], P('mp')
- w_query_grad: float32 [1280, 256], P('dp', 'mp')
- w_key_grad: float32 [768, 256], P('dp', 'mp')
- w_value_grad: float32 [768, 1280], P('dp', 'mp')
- w_out_grad: float32 [1280, 1280], P('mp', 'dp')
- w_one_grad: float32 [1280, 1280], P('dp', 'mp')
- w_two_grad: float32 [1280, 1280], P('mp', 'dp')
Inputs may be any that keep to these rules, and one draw needn't show every extreme that they name: The lengths[i] live slots of item i come first; later slots are padding. In every draw some item is full.
All inputs are finite; a program needn't handle non-finite values.
Results may differ from a plain program's by a relative error of at most 0.012.
The roundings to bfloat16 on the way count: a program that leaves them out, or rounds other values in their place, can miss the bound.
Values sent between devices are 32-bit elements; how exact they have to be, the bound alone decides.
No kernel may reach another device: no remote copies, remote signals or barrier semaphores. Data moves between devices by JAX's collectives and lax.ppermute only.
A program may use at most 320 MiB of HBM per device.

v0:
```python
import jax
import jax.numpy as jnp
from jax import lax
from jax.sharding import PartitionSpec as P

HEADS = 8


EPSILON = 1e-05
MASKED = -1e30


def norm_parts(tensor):
    centered = tensor - jnp.mean(tensor, axis=-1, keepdims=True)
    inv_std = lax.rsqrt(jnp.mean(centered * centered, axis=-1, keepdims=True) + EPSILON)
    return (centered * inv_std, inv_std)


def norm_back(upstream, unit_rows, inv_std, gain_vec):
    scaled = upstream * gain_vec
    row_mean = jnp.mean(scaled, axis=-1, keepdims=True)
    row_cross = jnp.mean(scaled * unit_rows, axis=-1, keepdims=True)
    return inv_std * (scaled - row_mean - unit_rows * row_cross)


def exact_gelu(tensor):
    return jax.nn.gelu(tensor, approximate=False)


def contract(form, first_op, second_op):
    return jnp.einsum(form, first_op, second_op, preferred_element_type=jnp.float32)


def table_sum(byte_hits, grads):
    upper = grads.astype(jnp.bfloat16)
    lower = (grads - upper.astype(jnp.float32)).astype(jnp.bfloat16)
    return contract("isv,isd->vd", byte_hits, upper) + contract("isv,isd->vd", byte_hits, lower)


def body(
    byte_ids,
    lengths,
    latents,
    byte_table,
    pos_table,
    gain_in,
    gain_lat,
    gain_mlp,
    w_query,
    w_key,
    w_value,
    w_out,
    w_one,
    w_two,
    out_grad,
):
    item_count, slot_count = byte_ids.shape
    vocab_size, width_in = byte_table.shape
    width_lat = latents.shape[2]
    local_heads = HEADS // lax.axis_size("mp")
    qk_cols = w_query.shape[1]
    qk_size = qk_cols // local_heads
    val_cols = w_value.shape[1]
    head_size = val_cols // local_heads
    factor = qk_size ** (-0.5)
    one_hot = byte_ids[:, :, None] == lax.iota(jnp.int32, vocab_size)[None, None, :]
    byte_hits = one_hot.astype(jnp.bfloat16)
    inputs = contract("isv,vd->isd", byte_hits, byte_table) + pos_table.astype(jnp.float32)[None]
    unit_in, inv_in = norm_parts(inputs)
    normed_in = (unit_in * gain_in).astype(jnp.bfloat16)
    key_rows = contract("isd,dc->isc", normed_in, w_key).astype(jnp.bfloat16)
    value_rows = contract("isd,dc->isc", normed_in, w_value).astype(jnp.bfloat16)
    lat_rows = latents.astype(jnp.float32)
    unit_lat, inv_lat = norm_parts(lat_rows)
    normed_lat = (unit_lat * gain_lat).astype(jnp.bfloat16)
    queries = contract("iqd,dc->iqc", normed_lat, w_query).astype(jnp.bfloat16)
    query_heads = queries.reshape(item_count, -1, local_heads, qk_size)
    key_heads = key_rows.reshape(item_count, slot_count, local_heads, qk_size)
    value_heads = value_rows.reshape(item_count, slot_count, local_heads, head_size)
    live_keys = lax.iota(jnp.int32, slot_count)[None, :] < lengths[:, None]

    def scores_of():
        raw_scores = contract("iqhd,ikhd->ihqk", query_heads, key_heads) * factor
        return jnp.where(live_keys[:, None, None, :], raw_scores, MASKED)

    scores = scores_of()
    row_max = jnp.max(scores, axis=-1, keepdims=True)
    raised = jnp.exp(scores - row_max)
    row_total = jnp.sum(raised, axis=-1, keepdims=True)
    weights = (raised / row_total).astype(jnp.bfloat16)
    log_total = row_max + jnp.log(row_total)
    attended = (
        contract("ihqk,ikhd->iqhd", weights, value_heads)
        .astype(jnp.bfloat16)
        .reshape(item_count, -1, val_cols)
    )
    mixed = lax.psum(contract("iqc,cd->iqd", attended, w_out), "mp")
    hidden = lat_rows + mixed
    unit_mlp, inv_mlp = norm_parts(hidden)
    normed_mlp = (unit_mlp * gain_mlp).astype(jnp.bfloat16)
    up_proj = contract("iqd,dc->iqc", normed_mlp, w_one)
    act_value, gelu_pull = jax.vjp(exact_gelu, up_proj)
    activated = act_value.astype(jnp.bfloat16)
    branch = lax.psum(contract("iqc,cd->iqd", activated, w_two), "mp")
    latents_out = (hidden + branch).astype(jnp.bfloat16)
    act_grad = contract("iqd,cd->iqc", out_grad, w_two)
    w_two_grad = contract("iqc,iqd->cd", activated, out_grad)
    up_grad = gelu_pull(act_grad)[0].astype(jnp.bfloat16)
    w_one_grad = contract("iqd,iqc->dc", normed_mlp, up_grad)
    mlp_norm_grad = lax.psum(contract("iqc,dc->iqd", up_grad, w_one), "mp")
    gain_mlp_grad = jnp.sum(mlp_norm_grad * unit_mlp, axis=(0, 1))
    hidden_grad = out_grad.astype(jnp.float32) + norm_back(
        mlp_norm_grad, unit_mlp, inv_mlp, gain_mlp
    )
    mixed_grad = hidden_grad.astype(jnp.bfloat16)
    w_out_grad = contract("iqc,iqd->cd", attended, mixed_grad)
    attended_grad = contract("iqd,cd->iqc", mixed_grad, w_out).astype(jnp.bfloat16)
    attended_grad = attended_grad.reshape(item_count, -1, local_heads, head_size)
    recomputed = jnp.exp(scores_of() - log_total)
    weights_grad = contract("iqhd,ikhd->ihqk", attended_grad, value_heads)
    row_delta = jnp.sum(recomputed * weights_grad, axis=-1, keepdims=True)
    scores_grad = (recomputed * (weights_grad - row_delta)).astype(jnp.bfloat16)
    query_grad = (
        (contract("ihqk,ikhd->iqhd", scores_grad, key_heads) * factor)
        .astype(jnp.bfloat16)
        .reshape(item_count, -1, qk_cols)
    )
    key_grad = (
        (contract("ihqk,iqhd->ikhd", scores_grad, query_heads) * factor)
        .astype(jnp.bfloat16)
        .reshape(item_count, slot_count, qk_cols)
    )
    value_grad = (
        contract("ihqk,iqhd->ikhd", recomputed.astype(jnp.bfloat16), attended_grad)
        .astype(jnp.bfloat16)
        .reshape(item_count, slot_count, val_cols)
    )
    w_query_grad = contract("iqd,iqc->dc", normed_lat, query_grad)
    lat_norm_grad = lax.psum(contract("iqc,dc->iqd", query_grad, w_query), "mp")
    gain_lat_grad = jnp.sum(lat_norm_grad * unit_lat, axis=(0, 1))
    latent_grad = hidden_grad + norm_back(lat_norm_grad, unit_lat, inv_lat, gain_lat)
    w_key_grad = contract("isd,isc->dc", normed_in, key_grad)
    w_value_grad = contract("isd,isc->dc", normed_in, value_grad)
    in_norm_grad = contract("isc,dc->isd", key_grad, w_key) + contract(
        "isc,dc->isd", value_grad, w_value
    )
    col_share = width_in // lax.axis_size("mp")
    col_start = lax.axis_index("mp") * col_share
    cols_grad = lax.psum_scatter(in_norm_grad, "mp", scatter_dimension=2, tiled=True)
    unit_cols = lax.dynamic_slice_in_dim(unit_in, col_start, col_share, 2)
    gain_cols = lax.dynamic_slice_in_dim(gain_in, col_start, col_share, 0)
    scaled = cols_grad * gain_cols
    sum_plain, sum_cross = lax.psum(
        (
            jnp.sum(scaled, axis=-1, keepdims=True),
            jnp.sum(scaled * unit_cols, axis=-1, keepdims=True),
        ),
        "mp",
    )
    inputs_grad = inv_in * (scaled - sum_plain / width_in - unit_cols * (sum_cross / width_in))
    byte_part = table_sum(byte_hits, inputs_grad)
    pos_part = jnp.sum(inputs_grad, axis=0)
    gain_in_part = jnp.sum(cols_grad * unit_cols, axis=(0, 1))
    lat_share = width_lat // lax.axis_size("mp")
    lat_start = lax.axis_index("mp") * lat_share
    gain_lat_part = lax.dynamic_slice_in_dim(gain_lat_grad, lat_start, lat_share, 0)
    gain_mlp_part = lax.dynamic_slice_in_dim(gain_mlp_grad, lat_start, lat_share, 0)
    col_sums = (
        lax.psum_scatter(w_query_grad, "dp", scatter_dimension=0, tiled=True),
        lax.psum_scatter(w_key_grad, "dp", scatter_dimension=0, tiled=True),
        lax.psum_scatter(w_value_grad, "dp", scatter_dimension=0, tiled=True),
        lax.psum_scatter(w_one_grad, "dp", scatter_dimension=0, tiled=True),
        lax.psum_scatter(pos_part, "dp", scatter_dimension=0, tiled=True),
    )
    row_sums = (
        lax.psum_scatter(w_out_grad, "dp", scatter_dimension=1, tiled=True),
        lax.psum_scatter(w_two_grad, "dp", scatter_dimension=1, tiled=True),
    )
    small_sums = lax.psum((byte_part, gain_in_part, gain_lat_part, gain_mlp_part), "dp")
    return (
        latents_out,
        latent_grad,
        small_sums[0],
        col_sums[4],
        small_sums[1],
        small_sums[2],
        small_sums[3],
        col_sums[0],
        col_sums[1],
        col_sums[2],
        row_sums[0],
        col_sums[3],
        row_sums[1],
    )


def solution(mesh):
    return jax.shard_map(
        body,
        mesh=mesh,
        in_specs=(
            P("dp", None),
            P("dp"),
            P("dp", None, None),
            P(),
            P(),
            P(),
            P(),
            P(),
            P(None, "mp"),
            P(None, "mp"),
            P(None, "mp"),
            P("mp", None),
            P(None, "mp"),
            P("mp", None),
            P("dp", None, None),
        ),
        out_specs=(
            P("dp", None, None),
            P("dp", None, None),
            P(None, "mp"),
            P("dp", "mp"),
            P("mp"),
            P("mp"),
            P("mp"),
            P("dp", "mp"),
            P("dp", "mp"),
            P("dp", "mp"),
            P("mp", "dp"),
            P("dp", "mp"),
            P("mp", "dp"),
        ),
        check_vma=False,
    )
```

profile of v0, /device:TPU:0, one launch (start us, length us, event | category | flops | bytes accessed | tf_op | source)
XLA Modules:
  0.0 1376.4 jit_solution(15900619418467890839)
XLA Ops:
  12.7 17.2 %add_reduce_fusion = (f32[4,2048]{1,0:T(4,128)S(1)}, f32[4,2048,768]{1,2,0:T(8,128)}) fusion(f32[2048,768]{0,1:T(8,128)} %copy.35, bf16[262,768]{1,0:T(8,128)(2,1)S(1)} %copy-done.27, s32[4,2048]{1,0:T(4,128)S(1)} %copy-done.23), kind=kOutput, calls=%fused_computation.3 | convolution fusion | flops 3311443968 | bytes 31925248 | tf_op jit(solution)/shard_map/isv,vd->isd/dot_general | solution.py:31
  30.0 13.3 multiply_reduce_fusion
  48.0 15.3 %multiply_convert_fusion = (bf16[4,2048,768]{1,2,0:T(8,128)(2,1)}, f32[4,2048,768]{1,2,0:T(8,128)}) fusion(f32[768]{0:T(1024)S(1)} %copy-done.52, f32[4,2048]{1,0:T(4,128)S(1)} %add_rsqrt_fusion, f32[4,2048]{1,0:T(4,128)S(1)} %broadcast_multiply_fusion, f32[4,2048,768]{1,2,0:T(8,128)S(1)} %copy-done.3, f32[2048,768]{0,1:T(8,128)} %copy.35), kind=kLoop, calls=%fused_computation | loop fusion | flops 31457280 | bytes 69274624 | tf_op jit(solution)/shard_map/convert_element_type | solution.py:70
  63.3 11.1 convolution_convert_fusion
  99.3 105.1 %all-reduce.9.cloned.1.call-done = f32[4,256,1280]{2,1,0:T(8,128)} async-done(((f32[4,256,1280]{2,1,0:T(8,128)}), f32[4,256,1280]{2,1,0:T(8,128)}) %all-reduce.9.cloned.1.call-update) | async-done | bytes 5242896 | tf_op jit(solution)/shard_map/psum | solution.py:97
  221.1 101.6 %all-reduce.11.cloned.1.call-done = f32[4,256,1280]{2,1,0:T(8,128)} async-done(((f32[4,256,1280]{2,1,0:T(8,128)}), f32[4,256,1280]{2,1,0:T(8,128)}) %all-reduce.11.cloned.1.call-update) | async-done | bytes 5242896 | tf_op jit(solution)/shard_map/psum | solution.py:110
  336.5 12.2 multiply_reduce_fusion.1
  348.6 9.4 fusion.26
  358.1 17.9 %fusion.63 = f32[4,2048,768]{1,2,0:T(8,128)} fusion(bf16[4,2048,320]{1,2,0:T(8,128)(2,1)} %bitcast.118, bf16[768,320]{0,1:T(8,128)(2,1)S(1)} %copy-done.26), kind=kOutput, calls=%fused_computation.109 | convolution fusion | flops 4026531840 | bytes 30900224 | tf_op jit(solution)/shard_map/isc,dc->isd/dot_general | solution.py:31
  376.1 10.9 multiply_convert_fusion.1
  392.9 16.2 %convolution_add_fusion = f32[4,2048,768]{1,2,0:T(8,128)} fusion(f32[4,2048,768]{1,2,0:T(8,128)} %fusion.63, bf16[4,2048,64]{1,2,0:T(8,128)(2,1)S(1)} %bitcast.122, bf16[768,64]{0,1:T(8,128)(2,1)S(1)} %copy-done.28), kind=kOutput, calls=%fused_computation.16 | convolution fusion | flops 811597824 | bytes 51478528 | tf_op jit(solution)/shard_map/isc,dc->isd/dot_general | solution.py:31
  409.9 179.9 %reduce-scatter.13.cloned.1.call-done = f32[4,2048,192]{1,2,0:T(8,128)} async-done(((f32[4,2048,768]{1,2,0:T(8,128)}), f32[4,2048,192]{1,2,0:T(8,128)}) %reduce-scatter.13.cloned.1.call-update) | async-done | bytes 6291472 | tf_op jit(solution)/shard_map/reduce_scatter | solution.py:149
  596.4 9.0 convolution_bitcast_fusion.5
  632.7 12.0 convolution_bitcast_fusion.4
  664.9 27.4 %reduce-scatter.27.cloned.1.call-done = f32[96,64]{1,0:T(8,128)} async-done(((f32[768,64]{1,0:T(8,128)}), f32[96,64]{1,0:T(8,128)}) %reduce-scatter.27.cloned.1.call-update) | async-done | bytes 24592
  693.7 63.3 %reduce-scatter.25.cloned.1.call-done = f32[160,64]{1,0:T(8,128)} async-done(((f32[1280,64]{1,0:T(8,128)}), f32[160,64]{1,0:T(8,128)}) %reduce-scatter.25.cloned.1.call-update) | async-done | bytes 40976
  758.7 187.9 %all-reduce.17.cloned.1.call-done = (f32[4,256,1280]{2,1,0:T(8,128)}, f32[4,256,1280]{2,1,0:T(8,128)}) async-done(((f32[4,256,1280]{2,1,0:T(8,128)}, f32[4,256,1280]{2,1,0:T(8,128)}), (f32[4,256,1280]{2,1,0:T(8,128)}, f32[4,256,1280]{2,1,0:T(8,128)})) %all-reduce.17.cloned.1.call-update) | async-done | bytes 10485776 | tf_op jit(solution)/shard_map/psum | solution.py:104
  960.9 22.5 %all-reduce = (f32[192]{0:T(256)}, f32[320]{0:T(512)}, f32[320]{0:T(512)}) all-reduce(f32[192]{0:T(256)S(1)} %get-tuple-element.13, f32[320]{0:T(512)S(1)} %dynamic_slice.14, f32[320]{0:T(512)S(1)} %dynamic_slice.15), channel_id=1, replica_groups=mesh['dp'=8,'mp'=4] {'dp'}, use_global_device_ids=true, to_apply=%region_26.27 | all-reduce | flops 832 | bytes 6656 | tf_op jit(solution)/shard_map/psum | solution.py:179
  983.4 34.6 %reduce-scatter.21.cloned.1.call-done = f32[160,320]{1,0:T(8,128)} async-done(((f32[1280,320]{1,0:T(8,128)}), f32[160,320]{1,0:T(8,128)}) %reduce-scatter.21.cloned.1.call-update) | async-done | bytes 204816 | tf_op jit(solution)/shard_map/reduce_scatter | solution.py:172
  1018.0 69.7 %reduce-scatter.23.cloned.1.call-done = f32[320,160]{0,1:T(8,128)} async-done(((f32[320,1280]{0,1:T(8,128)}), f32[320,160]{0,1:T(8,128)}) %reduce-scatter.23.cloned.1.call-update) | async-done | bytes 204816 | tf_op jit(solution)/shard_map/reduce_scatter | solution.py:177
  1087.7 67.4 %reduce-scatter.17.cloned.1.call-done = f32[96,320]{1,0:T(8,128)} async-done(((f32[768,320]{1,0:T(8,128)}), f32[96,320]{1,0:T(8,128)}) %reduce-scatter.17.cloned.1.call-update) | async-done | bytes 122896 | tf_op jit(solution)/shard_map/reduce_scatter | solution.py:171
  1155.1 70.3 %reduce-scatter.19.cloned.1.call-done = f32[320,160]{0,1:T(8,128)} async-done(((f32[320,1280]{0,1:T(8,128)}), f32[320,160]{0,1:T(8,128)}) %reduce-scatter.19.cloned.1.call-update) | async-done | bytes 204816 | tf_op jit(solution)/shard_map/reduce_scatter | solution.py:176
  1225.4 73.3 %all-reduce.13.cloned.1.call-done = f32[262,192]{1,0:T(8,128)} async-done(((f32[262,192]{1,0:T(8,128)}), f32[262,192]{1,0:T(8,128)}) %all-reduce.13.cloned.1.call-update) | async-done | bytes 201232 | tf_op jit(solution)/shard_map/psum | solution.py:179
  1298.7 69.1 %reduce-scatter.15.cloned.1.call-done = f32[256,192]{0,1:T(8,128)} async-done(((f32[2048,192]{0,1:T(8,128)}), f32[256,192]{0,1:T(8,128)}) %reduce-scatter.15.cloned.1.call-update) | async-done | bytes 196624 | tf_op jit(solution)/shard_map/reduce_scatter | solution.py:173
  (211 shorter events, 144.6 us)
Async XLA Ops:
  7.2 201.1 %copy-start = (bf16[1280,320]{0,1:T(8,128)(2,1)S(1)}, bf16[1280,320]{0,1:T(8,128)(2,1)}, u32[]{:S(2)}) copy-start(bf16[1280,320]{0,1:T(8,128)(2,1)} %param.27) | copy-start | bytes 2457604
  7.2 197.3 %all-reduce.9.cloned.1.call-start = ((), (), s32[]{:S(2)}) async-start(), calls=%async_computation.8 | async-start | bytes 10485760 | tf_op jit(solution)/shard_map/psum | solution.py:97
  43.9 32.9 %copy-start.37 = (f32[4,256]{1,0:T(4,128)}, f32[4,256]{1,0:T(4,128)S(1)}, u32[]{:S(2)}) copy-start(f32[4,256]{1,0:T(4,128)S(1)} %broadcast_multiply_fusion.6) | copy-start | bytes 12292
  48.0 28.8 %copy-start.42 = (f32[4,256]{1,0:T(4,128)}, f32[4,256]{1,0:T(4,128)S(1)}, u32[]{:S(2)}) copy-start(f32[4,256]{1,0:T(4,128)S(1)} %add_rsqrt_fusion.2) | copy-start | bytes 12292
  93.7 110.8 %copy-start.8 = (bf16[4,256,1280]{2,1,0:T(8,128)(2,1)S(1)}, bf16[4,256,1280]{2,1,0:T(8,128)(2,1)}, u32[]{:S(2)}) copy-start(bf16[4,256,1280]{2,1,0:T(8,128)(2,1)} %param.17) | copy-start | bytes 7864324
  99.1 223.7 %all-reduce.11.cloned.1.call-start = ((), (), s32[]{:S(2)}) async-start(), calls=%async_computation.9 | async-start | bytes 10485760 | tf_op jit(solution)/shard_map/psum | solution.py:110
  219.8 102.9 %copy-start.35 = (f32[4,256]{1,0:T(4,128)S(1)}, f32[4,256]{1,0:T(4,128)}, u32[]{:S(2)}) copy-start(f32[4,256]{1,0:T(4,128)} %copy-done.34) | copy-start | bytes 12292
  219.8 102.9 %copy-start.40 = (f32[4,256]{1,0:T(4,128)S(1)}, f32[4,256]{1,0:T(4,128)}, u32[]{:S(2)}) copy-start(f32[4,256]{1,0:T(4,128)} %copy-done.39) | copy-start | bytes 12292
  219.8 102.9 %copy-start.45 = (f32[1280]{0:T(1024)S(1)}, f32[1280]{0:T(1024)}, u32[]{:S(2)}) copy-start(f32[1280]{0:T(1024)} %param.22) | copy-start | bytes 15364
  219.9 370.0 %reduce-scatter.13.cloned.1.call-start = ((), (), s32[]{:S(2)}) async-start(), calls=%async_computation.10 | async-start | bytes 31457280 | tf_op jit(solution)/shard_map/reduce_scatter | solution.py:149
  221.1 107.4 %copy-start.36 = (f32[4,256]{1,0:T(4,128)S(1)}, f32[4,256]{1,0:T(4,128)}, u32[]{:S(2)}) copy-start(f32[4,256]{1,0:T(4,128)} %copy-done.34) | copy-start | bytes 12292
  221.1 107.4 %copy-start.41 = (f32[4,256]{1,0:T(4,128)S(1)}, f32[4,256]{1,0:T(4,128)}, u32[]{:S(2)}) copy-start(f32[4,256]{1,0:T(4,128)} %copy-done.39) | copy-start | bytes 12292
  409.1 241.4 %all-reduce.15.cloned.1.call-start = ((), (), s32[]{:S(2)}) async-start(), calls=%async_computation.19 | async-start | bytes 131072 | tf_op jit(solution)/shard_map/psum | solution.py:153
  596.3 95.9 %reduce-scatter.27.cloned.1.call-start = ((), (), s32[]{:S(2)}) async-start(), calls=%async_computation.18 | async-start | bytes 442368
  605.4 151.7 %reduce-scatter.25.cloned.1.call-start = ((), (), s32[]{:S(2)}) async-start(), calls=%async_computation.17 | async-start | bytes 737280
  614.4 332.2 %all-reduce.17.cloned.1.call-start = ((), (), s32[]{:S(2)}) async-start(), calls=%async_computation.20 | async-start | bytes 20971520 | tf_op jit(solution)/shard_map/psum | solution.py:104
  623.0 395.0 %reduce-scatter.21.cloned.1.call-start = ((), (), s32[]{:S(2)}) async-start(), calls=%async_computation.15 | async-start | bytes 2211840 | tf_op jit(solution)/shard_map/reduce_scatter | solution.py:172
  629.6 458.1 %reduce-scatter.23.cloned.1.call-start = ((), (), s32[]{:S(2)}) async-start(), calls=%async_computation.16 | async-start | bytes 2211840 | tf_op jit(solution)/shard_map/reduce_scatter | solution.py:177
  632.6 522.5 %reduce-scatter.17.cloned.1.call-start = ((), (), s32[]{:S(2)}) async-start(), calls=%async_computation.13 | async-start | bytes 1327104 | tf_op jit(solution)/shard_map/reduce_scatter | solution.py:171
  644.7 580.6 %reduce-scatter.19.cloned.1.call-start = ((), (), s32[]{:S(2)}) async-start(), calls=%async_computation.14 | async-start | bytes 2211840 | tf_op jit(solution)/shard_map/reduce_scatter | solution.py:176
  650.5 648.2 %all-reduce.13.cloned.1.call-start = ((), (), s32[]{:S(2)}) async-start(), calls=%async_computation.11 | async-start | bytes 540672 | tf_op jit(solution)/shard_map/psum | solution.py:179
  663.9 287.2 %slice-start.4 = ((s8[5242880]{0:T(1024)(128)(4,1)}), s8[1048576]{0:T(1024)(128)(4,1)S(1)}, s32[]{:S(2)}) async-start(s8[5242880]{0:T(1024)(128)(4,1)} %bitcast.114), calls=%async_computation.25 | async-start | bytes 2097152
  664.0 703.8 %reduce-scatter.15.cloned.1.call-start = ((), (), s32[]{:S(2)}) async-start(), calls=%async_computation.12 | async-start | bytes 1769472 | tf_op jit(solution)/shard_map/reduce_scatter | solution.py:173
  951.2 418.2 %copy-start.1 = (bf16[1280,320]{0,1:T(8,128)(2,1)S(1)}, bf16[1280,320]{0,1:T(8,128)(2,1)}, u32[]{:S(2)}) copy-start(bf16[1280,320]{0,1:T(8,128)(2,1)} %param.27) | copy-start | bytes 2457604
  (53 other events, 396.7 us)
Sparse Core Ops, SparseCore 0:
  99.2 105.2 all-reduce.8
  220.0 102.7 all-reduce.10
  409.2 180.5 reduce-scatter.12
  596.4 31.1 all-reduce.14
  630.8 61.3 reduce-scatter.26
  695.9 61.0 reduce-scatter.24
  760.4 186.1 all-reduce.16
  951.1 66.8 reduce-scatter.20
  1022.0 65.6 reduce-scatter.22
  1091.9 63.1 reduce-scatter.16
  1159.6 65.7 reduce-scatter.18
  1229.2 69.4 all-reduce.12
  1303.1 64.6 reduce-scatter.14
where the time goes:
time: 1380 us
  waiting for transfers between devices  1050 us (76%)
  matrix products  172 us (12%)
  other arithmetic  91 us (7%)
  local copies, waits for them, and re-layouts  24 us (2%)
  blocking collectives  22.5 us (2%)
  between operations  15.1 us (1%)
    psum x1, waiting for transfers between devices, body(): branch = lax.psum(contract('iqc,cd->iqd', activated, w_two), 'mp')  188 us
    reduce_scatter x1, waiting for transfers between devices, body(): lax.psum_scatter(in_norm_grad, 'mp', scatter_dimension=2, tiled=True)  180 us
    dot_general x27, matrix products, contract(): jnp.einsum(form, first_op, second_op, preferred_element_type=jnp.float32)  172 us
    psum x1, waiting for transfers between devices, body(): mixed = lax.psum(contract('iqc,cd->iqd', attended, w_out), 'mp')  105 us
    psum x1, waiting for transfers between devices, body(): mlp_norm_grad = lax.psum(contract('iqc,dc->iqd', up_grad, w_one), 'mp')  102 us
    unnamed x15, waiting for transfers between devices  90.9 us
    psum x1, waiting for transfers between devices, body(): lax.psum((byte_part, gain_in_part, gain_lat_part, gain_mlp_part), 'dp')  73.3 us
    reduce_scatter x1, waiting for transfers between devices, body(): lax.psum_scatter(w_out_grad, 'dp', scatter_dimension=1, tiled=True)  70.3 us
  transfers between devices with their start and end apart: 13, of which 12 were waited for; matrix products, arithmetic and copies ran while one was open for 6% of the time, Pallas kernels for 0%

commit v1 on v0

v1 whole, which is shorter than its diff:
```python
import jax
import jax.numpy as jnp
from jax import lax
from jax.experimental import pallas as pl
from jax.experimental.pallas import tpu as pltpu
from jax.sharding import PartitionSpec as P

HEADS = 8


EPSILON = 1e-05
MASKED = -1e30


def norm_parts(tensor):
    centered = tensor - jnp.mean(tensor, axis=-1, keepdims=True)
    inv_std = lax.rsqrt(jnp.mean(centered * centered, axis=-1, keepdims=True) + EPSILON)
    return (centered * inv_std, inv_std)


def norm_back(upstream, unit_rows, inv_std, gain_vec):
    scaled = upstream * gain_vec
    row_mean = jnp.mean(scaled, axis=-1, keepdims=True)
    row_cross = jnp.mean(scaled * unit_rows, axis=-1, keepdims=True)
    return inv_std * (scaled - row_mean - unit_rows * row_cross)


def exact_gelu(tensor):
    return jax.nn.gelu(tensor, approximate=False)


def contract(form, first_op, second_op):
    return jnp.einsum(form, first_op, second_op, preferred_element_type=jnp.float32)


def swap(tensor, axis, bit):
    return lax.ppermute(tensor, axis, [(i, i ^ bit) for i in range(lax.axis_size(axis))])


def arrange_kernel(place_ref, own_ref, core_ref, far_ref, far_core_ref, out_ref):
    place = place_ref[0]
    for step, ref in enumerate((own_ref, core_ref, far_ref, far_core_ref)):
        out_ref[place ^ step] = ref[...].astype(out_ref.dtype)


def gather_mp(own):
    rows, cols = own.shape
    core = swap(own, "mp", 1)
    far = swap(own, "mp", 2)
    far_core = swap(far, "mp", 1)
    place = lax.axis_index("mp").astype(jnp.int32).reshape(1)
    return pl.pallas_call(
        arrange_kernel,
        out_shape=jax.ShapeDtypeStruct((4, rows, cols), jnp.bfloat16),
        in_specs=[pl.BlockSpec(memory_space=pltpu.SMEM)] + [pl.BlockSpec(memory_space=pltpu.VMEM)] * 4,
        out_specs=pl.BlockSpec(memory_space=pltpu.VMEM),
        compiler_params=pltpu.CompilerParams(vmem_limit_bytes=40 * 2**20),
    )(place, own, core, far, far_core)


def scatter_sum(blocks, axis):
    count = blocks.shape[0]
    place = lax.axis_index(axis)
    bit = 1
    while count > 1:
        split = blocks.reshape(count // 2, 2, *blocks.shape[1:])
        mine = (place // bit) % 2
        send = lax.dynamic_index_in_dim(split, 1 - mine, 1, False)
        keep = lax.dynamic_index_in_dim(split, mine, 1, False)
        blocks = keep + swap(send, axis, bit)
        count //= 2
        bit *= 2
    return blocks[0]


def sum_dp(tensor):
    bit = 1
    while bit < lax.axis_size("dp"):
        tensor = tensor + swap(tensor, "dp", bit)
        bit *= 2
    return tensor


def body(
    byte_ids,
    lengths,
    latents,
    byte_table,
    pos_table,
    gain_in,
    gain_lat,
    gain_mlp,
    w_query,
    w_key,
    w_value,
    w_out,
    w_one,
    w_two,
    out_grad,
):
    item_count, slot_count = byte_ids.shape
    vocab_size, width_in = byte_table.shape
    width_lat = latents.shape[2]
    local_heads = HEADS // lax.axis_size("mp")
    qk_cols = w_query.shape[1]
    qk_size = qk_cols // local_heads
    val_cols = w_value.shape[1]
    head_size = val_cols // local_heads
    factor = qk_size ** (-0.5)
    mp_place = lax.axis_index("mp")
    f32, bf16 = jnp.float32, jnp.bfloat16

    def whole_rows(own):
        stacked = gather_mp(own.astype(f32))
        return stacked.reshape(-1, own.shape[1])

    w_out_all = whole_rows(w_out)
    w_one_rows = whole_rows(w_one.T)
    w_two_all = whole_rows(w_two)
    w_query_rows = whole_rows(w_query.T)

    one_hot = byte_ids[:, :, None] == lax.iota(jnp.int32, vocab_size)[None, None, :]
    byte_hits = one_hot.astype(bf16)
    inputs = contract("isv,vd->isd", byte_hits, byte_table) + pos_table.astype(f32)[None]
    unit_in, inv_in = norm_parts(inputs)
    normed_in = (unit_in * gain_in).astype(bf16)
    unit_low = unit_in.astype(bf16)
    w_kv = jnp.concatenate([w_key, w_value], axis=1)
    kv_rows = contract("isd,dc->isc", normed_in, w_kv).astype(bf16)
    key_rows, value_rows = kv_rows[..., :qk_cols], kv_rows[..., qk_cols:]
    lat_rows = latents.astype(f32)
    unit_lat, inv_lat = norm_parts(lat_rows)
    normed_lat = (unit_lat * gain_lat).astype(bf16)
    queries = contract("iqd,dc->iqc", normed_lat, w_query).astype(bf16)
    query_heads = queries.reshape(item_count, -1, local_heads, qk_size)
    key_heads = key_rows.reshape(item_count, slot_count, local_heads, qk_size)
    value_heads = value_rows.reshape(item_count, slot_count, local_heads, head_size)
    live_keys = lax.iota(jnp.int32, slot_count)[None, :] < lengths[:, None]

    def scores_of():
        raw_scores = contract("iqhd,ikhd->ihqk", query_heads, key_heads) * factor
        return jnp.where(live_keys[:, None, None, :], raw_scores, MASKED)

    scores = scores_of()
    row_max = jnp.max(scores, axis=-1, keepdims=True)
    raised = jnp.exp(scores - row_max)
    row_total = jnp.sum(raised, axis=-1, keepdims=True)
    weights = (raised / row_total).astype(bf16)
    log_total = row_max + jnp.log(row_total)
    attended = (
        contract("ihqk,ikhd->iqhd", weights, value_heads).astype(bf16).reshape(item_count, -1, val_cols)
    )
    attended_all = gather_mp(attended.astype(f32).reshape(-1, val_cols)).reshape(4, item_count, -1, val_cols)
    attended_all = attended_all.transpose(1, 2, 0, 3).reshape(item_count, -1, width_lat)
    hidden = lat_rows + contract("iqc,cd->iqd", attended_all, w_out_all)
    unit_mlp, inv_mlp = norm_parts(hidden)
    normed_mlp = (unit_mlp * gain_mlp).astype(bf16)
    up_proj = contract("iqd,cd->iqc", normed_mlp, w_one_rows)
    act_value, gelu_pull = jax.vjp(exact_gelu, up_proj)
    activated = act_value.astype(bf16)
    latents_out = (hidden + contract("iqc,cd->iqd", activated, w_two_all)).astype(bf16)
    act_grad = contract("iqd,cd->iqc", out_grad, w_two_all)
    up_grad = gelu_pull(act_grad)[0].astype(bf16)
    mlp_norm_grad = contract("iqc,cd->iqd", up_grad, w_one_rows)
    gain_mlp_grad = jnp.sum(mlp_norm_grad * unit_mlp, axis=(0, 1))
    hidden_grad = out_grad.astype(f32) + norm_back(mlp_norm_grad, unit_mlp, inv_mlp, gain_mlp)
    mixed_grad = hidden_grad.astype(bf16)
    own_cols = lambda t: lax.dynamic_slice_in_dim(t, mp_place * val_cols, val_cols, 2)
    w_two_grad = contract("iqd,iqc->dc", out_grad, own_cols(activated))
    w_one_grad = contract("iqd,iqc->dc", normed_mlp, own_cols(up_grad))
    w_out_grad = contract("iqd,iqc->dc", mixed_grad, attended)
    dp_size = lax.axis_size("dp")

    def rows_dp(tensor):
        return scatter_sum(tensor.reshape(dp_size, -1, tensor.shape[1]), "dp")

    w_two_grad, w_one_grad, w_out_grad = rows_dp(w_two_grad), rows_dp(w_one_grad), rows_dp(w_out_grad)

    attended_grad = contract("iqd,cd->iqc", mixed_grad, w_out).astype(bf16)
    attended_grad = attended_grad.reshape(item_count, -1, local_heads, head_size)
    recomputed = jnp.exp(scores_of() - log_total)
    weights_grad = contract("iqhd,ikhd->ihqk", attended_grad, value_heads)
    row_delta = jnp.sum(recomputed * weights_grad, axis=-1, keepdims=True)
    scores_grad = (recomputed * (weights_grad - row_delta)).astype(bf16)
    query_grad = (contract("ihqk,ikhd->iqhd", scores_grad, key_heads) * factor).astype(bf16)
    query_grad = query_grad.reshape(item_count, -1, qk_cols)
    key_grad = (contract("ihqk,iqhd->ikhd", scores_grad, query_heads) * factor).astype(bf16)
    key_grad = key_grad.reshape(item_count, slot_count, qk_cols)
    value_grad = contract("ihqk,iqhd->ikhd", recomputed.astype(bf16), attended_grad).astype(bf16)
    value_grad = value_grad.reshape(item_count, slot_count, val_cols)
    w_query_grad = rows_dp(contract("iqd,iqc->dc", normed_lat, query_grad))
    query_all = gather_mp(query_grad.astype(f32).reshape(-1, qk_cols)).reshape(4, item_count, -1, qk_cols)
    query_all = query_all.transpose(1, 2, 0, 3).reshape(item_count, -1, qk_cols * 4)
    lat_norm_grad = contract("iqc,cd->iqd", query_all, w_query_rows)
    gain_lat_grad = jnp.sum(lat_norm_grad * unit_lat, axis=(0, 1))
    latent_grad = hidden_grad + norm_back(lat_norm_grad, unit_lat, inv_lat, gain_lat)
    kv_grad = jnp.concatenate([key_grad, value_grad], axis=2)
    unit_kv = contract("isd,isc->dc", unit_low, kv_grad)
    gain_in_grad = jnp.sum(unit_kv * w_kv.astype(f32), axis=1)
    kv_sum = rows_dp(unit_kv * gain_in[:, None])
    in_norm_grad = contract("isc,dc->isd", kv_grad, w_kv)
    inputs_grad = norm_back(in_norm_grad, unit_low.astype(f32), inv_in, gain_in)
    byte_part = contract("isv,isd->vd", byte_hits, inputs_grad.astype(bf16))
    pos_part = jnp.sum(inputs_grad, axis=0)
    both = jnp.concatenate([pos_part, byte_part, gain_in_grad[None]], axis=0)
    mine = scatter_sum(both.reshape(-1, 4, width_in // 4).transpose(1, 0, 2), "mp")
    pos_mine = rows_dp(mine[:slot_count])
    lat_share = width_lat // 4
    gains = jnp.stack([gain_lat_grad, gain_mlp_grad])
    gains = lax.dynamic_slice_in_dim(gains, mp_place * lat_share, lat_share, 1)
    byte_mine, gains = sum_dp(mine[slot_count:]), sum_dp(gains)
    return (
        latents_out,
        latent_grad,
        byte_mine[:vocab_size],
        pos_mine,
        byte_mine[vocab_size],
        gains[0],
        gains[1],
        w_query_grad,
        kv_sum[:, :qk_cols],
        kv_sum[:, qk_cols:],
        w_out_grad.T,
        w_one_grad,
        w_two_grad.T,
    )


def solution(mesh):
    return jax.shard_map(
        body,
        mesh=mesh,
        in_specs=(
            P("dp", None),
            P("dp"),
            P("dp", None, None),
            P(),
            P(),
            P(),
            P(),
            P(),
            P(None, "mp"),
            P(None, "mp"),
            P(None, "mp"),
            P("mp", None),
            P(None, "mp"),
            P("mp", None),
            P("dp", None, None),
        ),
        out_specs=(
            P("dp", None, None),
            P("dp", None, None),
            P(None, "mp"),
            P("dp", "mp"),
            P("mp"),
            P("mp"),
            P("mp"),
            P("dp", "mp"),
            P("dp", "mp"),
            P("dp", "mp"),
            P("mp", "dp"),
            P("dp", "mp"),
            P("mp", "dp"),
        ),
        check_vma=False,
    )
```

time: 1380 us -> 598 us (0.43)
  waiting for transfers between devices: 1050 us -> 154 us
  local copies, waits for them, and re-layouts: 24 us -> 107 us
  starting transfers between devices: 1.62 us -> 41.6 us
  blocking collectives: 22.5 us -> 0 us
    reduce_scatter x6 -> x0, waiting for transfers between devices: 491 us -> none  [the longest x1 180 us: body(): lax.psum_scatter(in_norm_grad, 'mp', scatter_dimension=2, tiled=True)]
    psum x5 -> x0, waiting for transfers between devices: 468 us -> none  [the longest x1 188 us: body(): branch = lax.psum(contract('iqc,cd->iqd', activated, w_two), 'mp')]
    ppermute x0 -> x44, waiting for transfers between devices: none -> 154 us  [swap(): lax.ppermute(tensor, axis, [(i, i ^ bit) for i in range(lax.axis_size(axi...]
    unnamed x15 -> x0, waiting for transfers between devices: 90.9 us -> none
    ppermute x0 -> x44, starting transfers between devices: none -> 41.6 us  [swap(): lax.ppermute(tensor, axis, [(i, i ^ bit) for i in range(lax.axis_size(axi...]
    psum x1 -> x0, blocking collectives: 22.5 us -> none  [body(): lax.psum((byte_part, gain_in_part, gain_lat_part, gain_mlp_part), 'dp')]
    reshape x0 -> x4, local copies, waits for them, and re-layouts: none -> 14.3 us  [the longest x1 8.12 us: body(): value_grad = value_grad.reshape(item_count, slot_count, val_cols)]
    dot_general x27 -> x23, matrix products: 172 us -> 179 us  [contract(): jnp.einsum(form, first_op, second_op, preferred_element_type=jnp.float32)]
  transfers between devices with their start and end apart: 13 -> 44, of which waited for: 12 -> 15; matrix products, arithmetic and copies ran while one was open for 6% -> 50% of each run, Pallas kernels for 0% -> 1%
where the time goes in v1:
time: 598 us; the launch traced here: 590 us
  matrix products  179 us (30%)
  waiting for transfers between devices  154 us (26%)
  local copies, waits for them, and re-layouts  107 us (18%)
  other arithmetic  95 us (16%)
  starting transfers between devices  41.6 us (7%)
  Pallas kernels  11.2 us (2%)
    dot_general x23, matrix products, contract(): jnp.einsum(form, first_op, second_op, preferred_element_type=jnp.float32)  179 us
    ppermute x44, waiting for transfers between devices, swap(): lax.ppermute(tensor, axis, [(i, i ^ bit) for i in range(lax.axis_size(axi...  154 us
    ppermute x44, starting transfers between devices, swap(): lax.ppermute(tensor, axis, [(i, i ^ bit) for i in range(lax.axis_size(axi...  41.6 us
    unnamed x147, local copies, waits for them, and re-layouts  26.3 us
    reduce_sum x1, other arithmetic, body(): pos_part = jnp.sum(inputs_grad, axis=0)  17.3 us
    convert_element_type x1, other arithmetic, body(): activated = act_value.astype(bf16)  12.7 us
    squeeze x19, local copies, waits for them, and re-layouts, scatter_sum(): send = lax.dynamic_index_in_dim(split, 1 - mine, 1, False)  12.6 us
    convert_element_type x1, other arithmetic, body(): scores_grad = (recomputed * (weights_grad - row_delta)).astype(bf16)  12.3 us
  transfers between devices with their start and end apart: 44, of which 15 were waited for; matrix products, arithmetic and copies ran while one was open for 50% of the time, Pallas kernels for 1%

profile of v1, /device:TPU:0, one launch (start us, length us, event | category | flops | bytes accessed | tf_op | source)
XLA Modules:
  0.0 590.0 jit_solution(14274847661475931749)
XLA Ops:
  12.4 17.3 %add_reduce_fusion = (f32[4,2048]{1,0:T(4,128)S(1)}, f32[4,2048,768]{1,2,0:T(8,128)}) fusion(f32[2048,768]{0,1:T(8,128)} %copy.137, bf16[262,768]{1,0:T(8,128)(2,1)S(1)} %copy-done, s32[4,2048]{1,0:T(4,128)S(1)} %copy-done.50), kind=kOutput, calls=%fused_computation.9 | convolution fusion | flops 3311443968 | bytes 31925248 | tf_op jit(solution)/shard_map/isv,vd->isd/dot_general | solution.py:33
  29.8 10.5 %multiply_reduce_fusion = f32[4,2048]{1,0:T(4,128)S(1)} fusion(f32[4,2048,768]{1,2,0:T(8,128)} %get-tuple-element.99, f32[4,2048]{1,0:T(4,128)S(1)} %broadcast_multiply_fusion.3, f32[2048,768]{0,1:T(8,128)S(1)} %copy-done.9), kind=kLoop, calls=%fused_computation.6 | loop fusion | flops 25157632 | bytes 31522816 | tf_op jit(solution)/shard_map/reduce_sum | solution.py:17
  40.4 16.0 %fusion.47 = bf16[4,2048,384]{1,2,0:T(8,128)(2,1)} fusion(f32[4,2048,768]{1,2,0:T(8,128)} %get-tuple-element.99, f32[768]{0:T(1024)S(1)} %copy-done.55, f32[4,2048]{1,0:T(4,128)S(1)} %add_rsqrt_fusion, f32[4,2048]{1,0:T(4,128)S(1)} %broadcast_multiply_fusion.3, f32[2048,768]{0,1:T(8,128)} %copy.137, bf16[768,384]{0,1:T(8,128)(2,1)S(1)} %constant_dynamic-update-slice_fusion), kind=kOutput, calls=%fused_computation.89 | convolution fusion | flops 4866441216 | bytes 38407168 | tf_op jit(solution)/shard_map/isd,dc->isc/dot_general | solution.py:33
  76.3 8.8 %bitcast_convert_fusion = (f32[4,256,2,160]{1,3,2,0:T(8,128)S(1)}, bf16[4,2,160,256]{3,2,1,0:T(8,128)(2,1)}) fusion(bf16[4,2048,2,160]{1,3,2,0:T(8,128)(2,1)S(1)} %bitcast.270, f32[4,2,256]{2,1,0:T(2,128)S(1)} %fusion.3, f32[4,2,256]{2,1,0:T(2,128)S(1)} %get-tuple-element.100, f32[4,2,256,2048]{3,2,1,0:T(8,128)} %copy-done.10, ...), kind=kOutput, calls=%fused_computation.132 | convolution fusion | flops 1363804160 | bytes 24010752 | tf_op jit(solution)/shard_map/ihqk,ikhd->iqhd/dot_general | solution.py:33
  89.9 33.6 %collective-permute-done.16.far_ref = f32[64,1280]{1,0:T(8,128)S(1)} collective-permute-done((f32[64,1280]{1,0:T(8,128)S(1)}, f32[64,1280]{1,0:T(8,128)S(1)}, u32[]{:S(2)}, u32[]{:S(2)}) %collective-permute-start.16) | collective-permute-done | bytes 327712 | tf_op jit(solution)/shard_map/ppermute | solution.py:37
  148.8 15.5 %collective-permute-done.10.far_ref = f32[320,1280]{1,0:T(8,128)} collective-permute-done((f32[320,1280]{1,0:T(8,128)}, f32[320,1280]{1,0:T(8,128)}, u32[]{:S(2)}, u32[]{:S(2)}) %collective-permute-start.10) | collective-permute-done | bytes 1638432 | tf_op jit(solution)/shard_map/ppermute | solution.py:37
  164.3 34.2 %collective-permute-done.7.far_ref = f32[320,1280]{1,0:T(8,128)} collective-permute-done((f32[320,1280]{1,0:T(8,128)}, f32[320,1280]{1,0:T(8,128)}, u32[]{:S(2)}, u32[]{:S(2)}) %collective-permute-start.7) | collective-permute-done | bytes 1638432 | tf_op jit(solution)/shard_map/ppermute | solution.py:37
  219.0 12.7 %multiply_convert_fusion.4 = (bf16[4,256,1280]{2,1,0:T(8,128)(2,1)}, f32[4,256,1280]{2,1,0:T(8,128)}) fusion(f32[4,256,1280]{2,1,0:T(8,128)S(1)} %get-tuple-element.106, u8[256,1280]{1,0:T(8,128)(4,1)S(1)} %get-tuple-element.87, u8[256,1280]{1,0:T(8,128)(4,1)S(1)} %get-tuple-element.86), kind=kLoop, calls=%fused_computation.71 | loop fusion | flops 91750400 | bytes 13762560 | tf_op jit(solution)/shard_map/convert_element_type | solution.py:160
  236.5 8.0 %fusion.39 = bf16[4,256,1280]{2,1,0:T(8,128)(2,1)} fusion(f32[4,256,1280]{2,1,0:T(8,128)} %get-tuple-element.94, bf16[1280,1280,1]{1,0,2:T(8,128)(2,1)S(1)} %bitcast.259, bf16[4,256,1280]{2,1,0:T(8,128)(2,1)S(1)} %copy-done.20, f32[4,256,1280]{2,1,0:T(8,128)S(1)} %copy-done.30), kind=kOutput, calls=%fused_computation.65 | convolution fusion | flops 3373793280 | bytes 19005440 | tf_op jit(solution)/shard_map/iqd,cd->iqc/dot_general | solution.py:33
  257.3 9.7 %fusion.50 = bf16[4,2,160,2048]{3,2,1,0:T(8,128)(2,1)} fusion(bf16[4,256,2,160]{1,3,2,0:T(8,128)(2,1)S(1)} %bitcast.296, f32[4,2,256]{2,1,0:T(2,128)S(1)} %bitcast.317, f32[4,2,256,2048]{3,2,1,0:T(8,128)} %copy-done.10, pred[4,2048]{1,0:T(4,128)(4,1)S(1)} %iota_compare_fusion.3), kind=kOutput, calls=%fused_computation.92 | convolution fusion | flops 1361575936 | bytes 22691840 | tf_op jit(solution)/shard_map/ihqk,iqhd->ikhd/dot_general | solution.py:33
  267.0 12.2 %multiply_reduce_fusion.2 = (f32[4,2,256]{2,1,0:T(2,128)S(1)}, f32[4,2,256,2048]{3,2,1,0:T(8,128)}) fusion(f32[4,2,256]{2,1,0:T(2,128)S(1)} %bitcast.318, f32[4,2,256,2048]{3,2,1,0:T(8,128)} %copy-done.10, pred[4,2048]{1,0:T(4,128)(4,1)S(1)} %iota_compare_fusion.3, bf16[4,256,2,160]{1,3,2,0:T(8,128)(2,1)S(1)} %bitcast.297, ...), kind=kOutput, calls=%fused_computation.12 | convolution fusion | flops 1363146752 | bytes 39477248 | tf_op jit(solution)/shard_map/iqhd,ikhd->ihqk/dot_general | solution.py:33
  279.2 12.3 %multiply_convert_fusion.2 = bf16[4,2,256,2048]{3,2,1,0:T(8,128)(2,1)S(1)} fusion(f32[4,2,256,2048]{3,2,1,0:T(8,128)} %get-tuple-element.109, f32[4,2,256]{2,1,0:T(2,128)S(1)} %get-tuple-element.108, f32[4,2,256]{2,1,0:T(2,128)S(1)} %bitcast.319, f32[4,2,256,2048]{3,2,1,0:T(8,128)} %copy-done.10, pred[4,2048]{1,0:T(4,128)(4,1)S(1)} %iota_compare_fusion.3), kind=kLoop, calls=%fused_computation.11 | loop fusion | flops 25165824 | bytes 41967616 | tf_op jit(solution)/shard_map/convert_element_type | solution.py:184
  300.7 8.1 %copy.152 = bf16[4,2048,320]{2,1,0:T(8,128)(2,1)} copy(bf16[4,2048,320]{1,2,0:T(8,128)(2,1)} %bitcast.281) | data formatting | bytes 10485760 | tf_op jit(solution)/shard_map/reshape | solution.py:190
  311.5 28.1 %multiply_reduce_fusion.1 = (f32[4,2048]{1,0:T(4,128)S(1)}, f32[4,2048]{1,0:T(4,128)S(1)}, bf16[4,2048,768]{1,2,0:T(8,128)(2,1)}, f32[4,2048,768]{1,2,0:T(8,128)}) fusion(f32[768]{0:T(1024)S(1)} %copy-done.55, f32[4,2048]{1,0:T(4,128)S(1)} %add_rsqrt_fusion, f32[4,2048]{1,0:T(4,128)S(1)} %broadcast_multiply_fusion.3, ...), kind=kOutput, calls=%fused_computation.10 | convolution fusion | flops 4901027840 | bytes 76221440 | tf_op jit(solution)/shard_map/isc,dc->isd/dot_general | solution.py:33
  339.6 13.5 %broadcast_multiply_fusion = (f32[768,384]{1,0:T(8,128)}, f32[768,384]{1,0:T(8,128)}) fusion(f32[768]{0:T(1024)S(1)} %copy-done.55, bf16[4,2048,768]{1,2,0:T(8,128)(2,1)} %get-tuple-element.92, bf16[4,2048,320]{2,1,0:T(8,128)(2,1)S(1)} %copy-done.17, bf16[4,2048,64]{2,1,0:T(8,128)(2,1)} %copy.151), kind=kOutput, calls=%fused_computation.137 | convolution fusion | flops 4844716032 | bytes 21236736 | tf_op jit(solution)/shard_map/isd,isc->dc/dot_general | solution.py:33
  353.2 17.0 %fusion.6 = f32[262,768,1]{0,1,2:T(8,128)} fusion(bf16[4,2048,768]{1,2,0:T(8,128)(2,1)} %get-tuple-element.92, f32[4,2048,768]{1,2,0:T(8,128)} %get-tuple-element.112, f32[4,2048]{1,0:T(4,128)S(1)} %broadcast_multiply_fusion.1, f32[4,2048]{1,0:T(4,128)S(1)} %broadcast_multiply_fusion.2, f32[768]{0:T(1024)S(1)} %copy-done.55, ...), kind=kOutput, calls=%fused_computation.20 | convolution fusion | flops 3342909440 | bytes 38687744 | tf_op jit(solution)/shard_map/isv,isd->vd/dot_general | solution.py:33
  370.2 17.3 %fusion.25 = f32[2048,768]{0,1:T(8,128)} fusion(f32[4,2048]{1,0:T(4,128)S(1)} %broadcast_multiply_fusion.1, bf16[4,2048,768]{1,2,0:T(8,128)(2,1)} %get-tuple-element.92, f32[4,2048]{1,0:T(4,128)S(1)} %broadcast_multiply_fusion.2, f32[4,2048,768]{1,2,0:T(8,128)} %get-tuple-element.112, f32[768]{0:T(1024)S(1)} %copy-done.55, f32[4,2048]{1,0:T(4,128)S(1)} %add_rsqrt_fusion), kind=kLoop, calls=%fused_computation.43 | loop fusion | flops 42467328 | bytes 44141568 | tf_op jit(solution)/shard_map/reduce_sum | solution.py:204
  412.3 8.3 %concatenate.21 = f32[2311,4,192]{0,2,1:T(8,128)} concatenate(f32[2048,4,192]{0,2,1:T(8,128)} %bitcast.269, f32[262,4,192]{0,2,1:T(8,128)} %bitcast.307, f32[1,4,192]{0,2,1:T(8,128)S(1)} %concatenate.22), dimensions={0} | concatenate | bytes 14198784 | tf_op jit(solution)/shard_map/concatenate | solution.py:205
  455.3 7.2 %fusion.30 = f32[4,256,1280]{2,1,0:T(8,128)} fusion(f32[4,256,1280]{2,1,0:T(8,128)} %copy-done.15, bf16[4,256,1280]{2,1,0:T(8,128)(2,1)S(1)} %copy-done.14, f32[4,256,1280,1]{2,1,0,3:T(8,128)} %copy-done.18, f32[4,256]{1,0:T(4,128)S(1)} %broadcast_multiply_fusion.4, f32[4,256]{1,0:T(4,128)S(1)} %broadcast_multiply_fusion.5, f32[1280]{0:T(1024)S(1)} %copy-done.61, ...), kind=kLoop, calls=%fused_computation.48 | loop fusion | flops 11796480 | bytes 18371584 | tf_op jit(solution)/shard_map/add | solution.py:196
  497.1 8.6 %collective-permute-done.35 = f32[4,160,320]{2,1,0:T(8,128)S(1)} collective-permute-done((f32[4,160,320]{2,1,0:T(8,128)S(1)}, f32[4,160,320]{2,1,0:T(8,128)S(1)}, u32[]{:S(2)}, u32[]{:S(2)}) %collective-permute-start.35) | collective-permute-done | bytes 819232 | tf_op jit(solution)/shard_map/ppermute | solution.py:37
  515.1 15.9 %collective-permute-done.19 = f32[1,2311,192]{1,2,0:T(8,128)} collective-permute-done((f32[1,2311,192]{1,2,0:T(8,128)}, f32[1,2311,192]{1,2,0:T(8,128)}, u32[]{:S(2)}, u32[]{:S(2)}) %collective-permute-start.19) | collective-permute-done | bytes 1774880 | tf_op jit(solution)/shard_map/ppermute | solution.py:37
  546.9 11.6 %collective-permute-done.23 = f32[4,256,192]{1,2,0:T(8,128)S(1)} collective-permute-done((f32[4,256,192]{1,2,0:T(8,128)S(1)}, f32[4,256,192]{1,2,0:T(8,128)S(1)}, u32[]{:S(2)}, u32[]{:S(2)}) %collective-permute-start.23) | collective-permute-done | bytes 786464 | tf_op jit(solution)/shard_map/ppermute | solution.py:37
  564.9 9.1 %collective-permute-done.21 = f32[263,192]{0,1:T(8,128)S(1)} collective-permute-done((f32[263,192]{0,1:T(8,128)S(1)}, f32[263,192]{0,1:T(8,128)S(1)}, u32[]{:S(2)}, u32[]{:S(2)}) %collective-permute-start.21) | collective-permute-done | bytes 202016 | tf_op jit(solution)/shard_map/ppermute | solution.py:37
  577.9 9.1 %collective-permute-done.22 = f32[263,192]{0,1:T(8,128)S(1)} collective-permute-done((f32[263,192]{0,1:T(8,128)S(1)}, f32[263,192]{0,1:T(8,128)S(1)}, u32[]{:S(2)}, u32[]{:S(2)}) %collective-permute-start.22) | collective-permute-done | bytes 202016 | tf_op jit(solution)/shard_map/ppermute | solution.py:37
  (352 shorter events, 243.3 us)
Async XLA Ops:
  3.1 124.2 %collective-permute-start.4 = (f32[320,1280]{1,0:T(8,128)}, f32[320,1280]{1,0:T(8,128)}, u32[]{:S(2)}, u32[]{:S(2)}) collective-permute-start(f32[320,1280]{1,0:T(8,128)} %convert_element_type.126.own_ref), channel_id=1, source_target_pairs={{0,2},{1,3},{2,0},{3,1},{4,6},{5,7},{6,4},{7,5},{8,10},{9,11},{10,... | collective-permute-start | bytes 4915208 | tf_op jit(solution)/shard_map/ppermute | solution.py:37
  86.2 39.4 %collective-permute-start.1 = (f32[1024,320]{0,1:T(8,128)S(1)}, f32[1024,320]{0,1:T(8,128)}, u32[]{:S(2)}, u32[]{:S(2)}) collective-permute-start(f32[1024,320]{0,1:T(8,128)S(1)} %bitcast.282), channel_id=1, source_target_pairs={{0,2},{1,3},{2,0},{3,1},{4,6},{5,7},{6,4},{7,5},{8,10},{9,11},{10,... | collective-permute-start | bytes 3932168 | tf_op jit(solution)/shard_map/ppermute | solution.py:37
  86.3 41.0 %collective-permute-start = (f32[1024,320]{0,1:T(8,128)S(1)}, f32[1024,320]{0,1:T(8,128)S(1)}, u32[]{:S(2)}, u32[]{:S(2)}) collective-permute-start(f32[1024,320]{0,1:T(8,128)S(1)} %bitcast.283), channel_id=1, source_target_pairs={{0,1},{1,0},{2,3},{3,2},{4,5},{5,4},{6,7},{7,6},{8,9},{9,8},{10,11... | collective-permute-start | bytes 3932168 | tf_op jit(solution)/shard_map/ppermute | solution.py:37
  86.4 37.1 %collective-permute-start.16 = (f32[64,1280]{1,0:T(8,128)S(1)}, f32[64,1280]{1,0:T(8,128)S(1)}, u32[]{:S(2)}, u32[]{:S(2)}) collective-permute-start(f32[64,1280]{1,0:T(8,128)S(1)} %convert_bitcast_fusion.2.own_ref), channel_id=1, source_target_pairs={{0,2},{1,3},{2,0},{3,1},{4,6},{5,7},{6,4},{7,5},{8,10},{9,11},{10,... | collective-permute-start | bytes 983048 | tf_op jit(solution)/shard_map/ppermute | solution.py:37
  88.4 36.4 %collective-permute-start.15 = (f32[64,1280]{1,0:T(8,128)S(1)}, f32[64,1280]{1,0:T(8,128)S(1)}, u32[]{:S(2)}, u32[]{:S(2)}) collective-permute-start(f32[64,1280]{1,0:T(8,128)S(1)} %convert_bitcast_fusion.2.own_ref), channel_id=1, source_target_pairs={{0,1},{1,0},{2,3},{3,2},{4,5},{5,4},{6,7},{7,6},{8,9},{9,8},{10,11... | collective-permute-start | bytes 983048 | tf_op jit(solution)/shard_map/ppermute | solution.py:37
  125.3 39.0 %collective-permute-start.10 = (f32[320,1280]{1,0:T(8,128)}, f32[320,1280]{1,0:T(8,128)}, u32[]{:S(2)}, u32[]{:S(2)}) collective-permute-start(f32[320,1280]{1,0:T(8,128)} %convert_element_type.131.own_ref), channel_id=1, source_target_pairs={{0,2},{1,3},{2,0},{3,1},{4,6},{5,7},{6,4},{7,5},{8,10},{9,11},{10,... | collective-permute-start | bytes 4915208 | tf_op jit(solution)/shard_map/ppermute | solution.py:37
  125.6 72.9 %collective-permute-start.7 = (f32[320,1280]{1,0:T(8,128)}, f32[320,1280]{1,0:T(8,128)}, u32[]{:S(2)}, u32[]{:S(2)}) collective-permute-start(f32[320,1280]{1,0:T(8,128)} %convert_bitcast_fusion.own_ref), channel_id=1, source_target_pairs={{0,2},{1,3},{2,0},{3,1},{4,6},{5,7},{6,4},{7,5},{8,10},{9,11},{10,... | collective-permute-start | bytes 4915208 | tf_op jit(solution)/shard_map/ppermute | solution.py:37
  127.4 71.2 %collective-permute-start.5 = (f32[320,1280]{1,0:T(8,128)}, f32[320,1280]{1,0:T(8,128)}, u32[]{:S(2)}, u32[]{:S(2)}) collective-permute-start(f32[320,1280]{1,0:T(8,128)} %collective-permute-done.4.far_ref), channel_id=1, source_target_pairs={{0,1},{1,0},{2,3},{3,2},{4,5},{5,4},{6,7},{7,6},{8,9},{9,8},{10,11... | collective-permute-start | bytes 4915208 | tf_op jit(solution)/shard_map/ppermute | solution.py:37
  136.1 95.6 %collective-permute-start.9 = (f32[320,1280]{1,0:T(8,128)}, f32[320,1280]{1,0:T(8,128)}, u32[]{:S(2)}, u32[]{:S(2)}) collective-permute-start(f32[320,1280]{1,0:T(8,128)} %convert_element_type.131.own_ref), channel_id=1, source_target_pairs={{0,1},{1,0},{2,3},{3,2},{4,5},{5,4},{6,7},{7,6},{8,9},{9,8},{10,11... | collective-permute-start | bytes 4915208 | tf_op jit(solution)/shard_map/ppermute | solution.py:37
  148.2 60.1 %collective-permute-start.6 = (f32[320,1280]{1,0:T(8,128)}, f32[320,1280]{1,0:T(8,128)S(1)}, u32[]{:S(2)}, u32[]{:S(2)}) collective-permute-start(f32[320,1280]{1,0:T(8,128)} %convert_bitcast_fusion.own_ref), channel_id=1, source_target_pairs={{0,1},{1,0},{2,3},{3,2},{4,5},{5,4},{6,7},{7,6},{8,9},{9,8},{10,11... | collective-permute-start | bytes 4915208 | tf_op jit(solution)/shard_map/ppermute | solution.py:37
  164.3 67.4 %collective-permute-start.11 = (f32[320,1280]{1,0:T(8,128)}, f32[320,1280]{1,0:T(8,128)S(1)}, u32[]{:S(2)}, u32[]{:S(2)}) collective-permute-start(f32[320,1280]{1,0:T(8,128)} %collective-permute-done.10.far_ref), channel_id=1, source_target_pairs={{0,1},{1,0},{2,3},{3,2},{4,5},{5,4},{6,7},{7,6},{8,9},{9,8},{10,11... | collective-permute-start | bytes 4915208 | tf_op jit(solution)/shard_map/ppermute | solution.py:37
  300.1 129.4 %collective-permute-start.13 = (f32[1024,64]{1,0:T(8,128)}, f32[1024,64]{1,0:T(8,128)}, u32[]{:S(2)}, u32[]{:S(2)}) collective-permute-start(f32[1024,64]{1,0:T(8,128)} %copy.149.own_ref), channel_id=1, source_target_pairs={{0,2},{1,3},{2,0},{3,1},{4,6},{5,7},{6,4},{7,5},{8,10},{9,11},{10,... | collective-permute-start | bytes 786440 | tf_op jit(solution)/shard_map/ppermute | solution.py:37
  300.4 131.6 %collective-permute-start.12 = (f32[1024,64]{1,0:T(8,128)}, f32[1024,64]{1,0:T(8,128)}, u32[]{:S(2)}, u32[]{:S(2)}) collective-permute-start(f32[1024,64]{1,0:T(8,128)} %copy.149.own_ref), channel_id=1, source_target_pairs={{0,1},{1,0},{2,3},{3,2},{4,5},{5,4},{6,7},{7,6},{8,9},{9,8},{10,11... | collective-permute-start | bytes 786440 | tf_op jit(solution)/shard_map/ppermute | solution.py:37
  401.7 77.3 %collective-permute-start.41 = (f32[4,160,320]{2,1,0:T(8,128)}, f32[4,160,320]{2,1,0:T(8,128)}, u32[]{:S(2)}, u32[]{:S(2)}) collective-permute-start(f32[4,160,320]{2,1,0:T(8,128)} %dynamic-slice_bitcast_fusion.1), channel_id=1, source_target_pairs={{0,4},{4,0},{8,12},{12,8},{16,20},{20,16},{24,28},{28,24},{1,5},{5... | collective-permute-start | bytes 2457608 | tf_op jit(solution)/shard_map/ppermute | solution.py:37
  411.1 54.1 %collective-permute-start.32 = (f32[4,96,384]{2,1,0:T(8,128)S(1)}, f32[4,96,384]{2,1,0:T(8,128)}, u32[]{:S(2)}, u32[]{:S(2)}) collective-permute-start(f32[4,96,384]{2,1,0:T(8,128)S(1)} %dynamic-slice_bitcast_fusion.4), channel_id=1, source_target_pairs={{0,4},{4,0},{8,12},{12,8},{16,20},{20,16},{24,28},{28,24},{1,5},{5... | collective-permute-start | bytes 1769480 | tf_op jit(solution)/shard_map/ppermute | solution.py:37
  424.8 62.5 %collective-permute-start.18 = (f32[2,2311,192]{1,2,0:T(8,128)}, f32[2,2311,192]{1,2,0:T(8,128)}, u32[]{:S(2)}, u32[]{:S(2)}) collective-permute-start(f32[2,2311,192]{1,2,0:T(8,128)} %dynamic-slice_bitcast_fusion), channel_id=1, source_target_pairs={{0,1},{1,0},{2,3},{3,2},{4,5},{5,4},{6,7},{7,6},{8,9},{9,8},{10,11... | collective-permute-start | bytes 10649096 | tf_op jit(solution)/shard_map/ppermute | solution.py:37
  462.4 24.8 %collective-permute-start.38 = (f32[4,160,320]{2,1,0:T(8,128)S(1)}, f32[4,160,320]{2,1,0:T(8,128)S(1)}, u32[]{:S(2)}, u32[]{:S(2)}) collective-permute-start(f32[4,160,320]{2,1,0:T(8,128)S(1)} %copy-done.47), channel_id=1, source_target_pairs={{0,4},{4,0},{8,12},{12,8},{16,20},{20,16},{24,28},{28,24},{1,5},{5... | collective-permute-start | bytes 2457608 | tf_op jit(solution)/shard_map/ppermute | solution.py:37
  463.8 41.9 %collective-permute-start.35 = (f32[4,160,320]{2,1,0:T(8,128)S(1)}, f32[4,160,320]{2,1,0:T(8,128)S(1)}, u32[]{:S(2)}, u32[]{:S(2)}) collective-permute-start(f32[4,160,320]{2,1,0:T(8,128)S(1)} %copy-done.46), channel_id=1, source_target_pairs={{0,4},{4,0},{8,12},{12,8},{16,20},{20,16},{24,28},{28,24},{1,5},{5... | collective-permute-start | bytes 2457608 | tf_op jit(solution)/shard_map/ppermute | solution.py:37
  481.3 28.5 %collective-permute-start.42 = (f32[2,160,320]{2,1,0:T(8,128)}, f32[2,160,320]{2,1,0:T(8,128)}, u32[]{:S(2)}, u32[]{:S(2)}) collective-permute-start(f32[2,160,320]{2,1,0:T(8,128)} %dynamic-slice_bitcast_fusion.5), channel_id=1, source_target_pairs={{0,8},{4,12},{8,0},{12,4},{16,24},{20,28},{24,16},{28,20},{1,9},{5... | collective-permute-start | bytes 1228808 | tf_op jit(solution)/shard_map/ppermute | solution.py:37
  493.1 37.9 %collective-permute-start.19 = (f32[1,2311,192]{1,2,0:T(8,128)}, f32[1,2311,192]{1,2,0:T(8,128)}, u32[]{:S(2)}, u32[]{:S(2)}) collective-permute-start(f32[1,2311,192]{1,2,0:T(8,128)} %constant_dynamic-slice_fusion.10), channel_id=1, source_target_pairs={{0,2},{1,3},{2,0},{3,1},{4,6},{5,7},{6,4},{7,5},{8,10},{9,11},{10,... | collective-permute-start | bytes 5324552 | tf_op jit(solution)/shard_map/ppermute | solution.py:37
  506.7 35.8 %collective-permute-start.36 = (f32[2,160,320]{2,1,0:T(8,128)}, f32[2,160,320]{2,1,0:T(8,128)}, u32[]{:S(2)}, u32[]{:S(2)}) collective-permute-start(f32[2,160,320]{2,1,0:T(8,128)} %dynamic-slice_bitcast_fusion.7), channel_id=1, source_target_pairs={{0,8},{4,12},{8,0},{12,4},{16,24},{20,28},{24,16},{28,20},{1,9},{5... | collective-permute-start | bytes 1228808 | tf_op jit(solution)/shard_map/ppermute | solution.py:37
  510.9 32.8 %collective-permute-start.43 = (f32[1,160,320]{2,1,0:T(8,128)S(1)}, f32[1,160,320]{2,1,0:T(8,128)}, u32[]{:S(2)}, u32[]{:S(2)}) collective-permute-start(f32[1,160,320]{2,1,0:T(8,128)S(1)} %constant_dynamic-slice_fusion.1), channel_id=1, source_target_pairs={{0,16},{4,20},{8,24},{12,28},{16,0},{20,4},{24,8},{28,12},{1,17},{... | collective-permute-start | bytes 614408 | tf_op jit(solution)/shard_map/ppermute | solution.py:37
  513.0 50.3 %collective-permute-start.40 = (f32[1,160,320]{2,1,0:T(8,128)S(1)}, f32[1,160,320]{2,1,0:T(8,128)}, u32[]{:S(2)}, u32[]{:S(2)}) collective-permute-start(f32[1,160,320]{2,1,0:T(8,128)S(1)} %constant_dynamic-slice_fusion.2), channel_id=1, source_target_pairs={{0,16},{4,20},{8,24},{12,28},{16,0},{20,4},{24,8},{28,12},{1,17},{... | collective-permute-start | bytes 614408 | tf_op jit(solution)/shard_map/ppermute | solution.py:37
  543.6 33.6 %collective-permute-start.37 = (f32[1,160,320]{2,1,0:T(8,128)S(1)}, f32[1,160,320]{2,1,0:T(8,128)S(1)}, u32[]{:S(2)}, u32[]{:S(2)}) collective-permute-start(f32[1,160,320]{2,1,0:T(8,128)S(1)} %constant_dynamic-slice_fusion.3), channel_id=1, source_target_pairs={{0,16},{4,20},{8,24},{12,28},{16,0},{20,4},{24,8},{28,12},{1,17},{... | collective-permute-start | bytes 614408 | tf_op jit(solution)/shard_map/ppermute | solution.py:37
  (91 other events, 925.9 us)
